TPU v7x, 32 devices: a whole 2x2x4 slice. The times are simulated.
32 devices in a mesh: grp: 4 (over z), src: 4 (over y, x), rcv: 2 (over core).
Axes of the slice: x: 2, y: 2, z: 4, core: 2. Of those that a mesh axis runs over, the one named last changes fastest.
Arguments:
- recorded: bfloat16 [4, 2, 4096, 4096], P('grp', None, 'src', 'rcv'), parts along dimension 0, as said below
- aperture: int32 [128, 32, 3], P(('grp', 'src'), 'rcv'), parts along dimension 0, may hold values from 0 to 32, as said below
Outputs:
- multiples: float32 [4, 2, 4096, 4096], P('grp', None, 'src', 'rcv'), parts along dimension 0
There are 4 independent parts, one for each index of `grp`. A program takes and returns all parts, laid end to end along the dimension named above; each array names one. Nothing has to cross between parts.
Inputs may be any that keep to these rules, and one draw needn't show every extreme that they name: The data obey reciprocity: recorded(f, c, q, j) equals recorded(f, c, j, q). `aperture`: field 1 is from 4 to 32, field 0 plus field 1 is at most 32, field 2 is from 0 to 2. In every draw some tile pair spans all 32 k-blocks and some has taper width 2.
All inputs are finite; a program needn't handle non-finite values.
Results may differ from a plain program's by a relative error of at most 0.0004.
Values may be sent and summed in bfloat16 or wider, within the bound.
A program may use at most 192 MiB of HBM per device.

v0:
```python
import jax
import jax.numpy as jnp
from jax import lax
from jax.sharding import PartitionSpec as P

NB = 32
TILE = 128


def tile_weights(aperture):
    block_ids = jnp.arange(NB, dtype=jnp.int32)
    offset = block_ids[None, None, :] - aperture[..., 0:1]
    extent = aperture[..., 1:2]
    taper_width = aperture[..., 2:3]
    margin = jnp.minimum(offset, extent - 1 - offset)
    ramped = jnp.minimum(
        1.0, (margin + 1).astype(jnp.float32) / (taper_width + 1).astype(jnp.float32)
    )
    return jnp.where((offset >= 0) & (offset < extent), ramped, 0.0)


def shards(recorded, aperture):
    slices = recorded.shape[0]
    own_rows = recorded.shape[2]
    own_cols = recorded.shape[3]
    row_tiles = own_rows // TILE
    col_tiles = own_cols // TILE
    weights = tile_weights(aperture)
    block_ids = jnp.arange(NB, dtype=jnp.int32)
    left_panel = lax.all_gather(recorded, "rcv", axis=3, tiled=True)

    def block_terms(incoming, first_row, span_rows, tile_weight):
        part_left = lax.dynamic_slice_in_dim(left_panel, first_row, span_rows, 3)
        part_left = part_left.reshape(slices, 2, row_tiles, TILE, span_rows)
        block_of = (first_row + jnp.arange(span_rows, dtype=jnp.int32)) // TILE
        row_weights = jnp.sum(
            jnp.where(block_of[:, None] == block_ids[None, :], tile_weight[:, :, None, :], 0.0),
            axis=-1,
        )
        scaled = (part_left[:, :, :, None, :, :] * row_weights[None, None, :, :, None, :]).astype(
            jnp.bfloat16
        )
        sub_tiles = tile_weight.shape[1]
        right_tiles = incoming.reshape(slices, 2, span_rows, sub_tiles, TILE)
        products = jnp.einsum(
            "fastik,fbktj->fabstij", scaled, right_tiles, preferred_element_type=jnp.float32
        )
        return jnp.stack(
            [products[:, 0, 0] - products[:, 1, 1], products[:, 0, 1] + products[:, 1, 0]], 1
        )

    empty = jnp.zeros((slices, 2, row_tiles, col_tiles, TILE, TILE), jnp.float32)
    incoming = lax.all_gather(recorded, "src", axis=2, tiled=True)
    extent = incoming.shape[2]

    def add_block(first_row, span_rows, running):
        portion = lax.dynamic_slice_in_dim(incoming, first_row, span_rows, 2)
        return running + block_terms(portion, first_row, span_rows, weights)

    sweeps = extent // TILE
    summed = lax.fori_loop(
        0, sweeps, lambda number, running: add_block(number * TILE, TILE, running), empty
    )
    return summed.transpose(0, 1, 2, 4, 3, 5).reshape(slices, 2, own_rows, own_cols)


def solution(mesh):
    in_specs = (P("grp", None, "src", "rcv"), P(("grp", "src"), "rcv", None))
    out_specs = P("grp", None, "src", "rcv")
    return jax.shard_map(shards, mesh=mesh, in_specs=in_specs, out_specs=out_specs, check_vma=False)
```

profile of v0, /device:TPU:1, one launch (start us, length us, event | category | flops | bytes accessed | tf_op | source)
XLA Modules:
  0.0 2203.3 jit_solution(10129408972959190159)
XLA Ops:
  19.4 22.1 %all-gather.5.cloned.1.call-done = bf16[1,2,1024,4096]{3,2,1,0:T(8,128)(2,1)} async-done(((bf16[1,2,1024,2048]{3,2,1,0:T(8,128)(2,1)}), bf16[1,2,1024,4096]{3,2,1,0:T(8,128)(2,1)}) %all-gather.5.cloned.1.call-update) | async-done | bytes 16777232 | tf_op jit(solution)/shard_map/all_gather | solution.py:30
  41.5 299.9 %all-gather.3.cloned.1.call-done = bf16[1,2,4096,2048]{2,3,1,0:T(8,128)(2,1)} async-done(((bf16[1,2,1024,2048]{2,3,1,0:T(8,128)(2,1)}), bf16[1,2,4096,2048]{2,3,1,0:T(8,128)(2,1)}) %all-gather.3.cloned.1.call-update) | async-done | bytes 33554448 | tf_op jit(solution)/shard_map/all_gather | solution.py:53
  341.4 1819.7 %while.16 = (s32[]{:T(128)}, f32[1,2,8,16,128,128]{4,5,2,3,1,0:T(8,128)}, bf16[1,2,4096,2048]{2,3,1,0:T(8,128)(2,1)}, bf16[1,2,1024,4096]{3,2,1,0:T(8,128)(2,1)}...) while((s32[]{:T(128)}, ...), condition=%wide.region_2.3_spmd.clone, body=%wide.region_0.2_spmd.clone.sunk | while | flops 2173995008 | bytes 141339840 | solution.py:61
  434.5 17.0 maximum_add_fusion.2
  491.4 17.0 maximum_add_fusion.2
  548.4 17.0 maximum_add_fusion.2
  605.4 17.0 maximum_add_fusion.2
  662.4 17.0 maximum_add_fusion.2
  719.4 17.0 maximum_add_fusion.2
  833.4 17.0 maximum_add_fusion.2
  890.3 17.0 maximum_add_fusion.2
  947.3 17.0 maximum_add_fusion.2
  1004.3 17.0 maximum_add_fusion.2
  1061.3 17.0 maximum_add_fusion.2
  1175.3 17.0 maximum_add_fusion.2
  1232.3 17.0 maximum_add_fusion.2
  1289.2 17.0 maximum_add_fusion.2
  1346.2 17.0 maximum_add_fusion.2
  1403.2 17.0 maximum_add_fusion.2
  1517.2 17.0 maximum_add_fusion.2
  1574.2 17.0 maximum_add_fusion.2
  1631.1 17.0 maximum_add_fusion.2
  2161.1 17.4 copy.16
  2178.5 18.0 reshape.136
  (374 shorter events, 1507.0 us)
Async XLA Ops:
  6.5 12.8 copy-start
  6.5 34.9 %all-gather.5.cloned.1.call-start = ((), (), s32[]{:S(2)}) async-start(), calls=%async_computation.1 | async-start | bytes 25165824 | tf_op jit(solution)/shard_map/all_gather | solution.py:30
  7.3 334.1 %all-gather.3.cloned.1.call-start = ((), (), s32[]{:S(2)}) async-start(), calls=%async_computation | async-start | bytes 41943040 | tf_op jit(solution)/shard_map/all_gather | solution.py:53
Sparse Core Ops, SparseCore 0:
  8.9 32.5 all-gather.4
  43.3 297.9 all-gather.2
where the time goes:
time: 2210 us; the launch traced here: 2200 us
  other arithmetic  1320 us (60%)
  matrix products  419 us (19%)
  waiting for transfers between devices  323 us (15%)
  local copies, waits for them, and re-layouts  124 us (6%)
    add x32, other arithmetic, add_block(): return running + block_terms(portion, first_row, span_rows, weights)  542 us
    dot_general x32, matrix products, block_terms(): jnp.einsum('fastik,fbktj->fabstij', scaled, right_tiles, preferred_elemen...  419 us
    sub x32, other arithmetic, block_terms(): products[:, 0, 0] - products[:, 1, 1]  377 us
    add x32, other arithmetic, block_terms(): products[:, 0, 1] + products[:, 1, 0]  374 us
    all_gather x1, waiting for transfers between devices, shards(): incoming = lax.all_gather(recorded, 'src', axis=2, tiled=True)  300 us
  transfers between devices with their start and end apart: 2, of which 2 were waited for; matrix products, arithmetic and copies ran while one was open for 1% of the time, Pallas kernels for 0%

commit v1 on v0

v1 whole, which is shorter than its diff:
```python
import functools

import jax
import jax.numpy as jnp
import numpy as np
from jax import lax
from jax.experimental import pallas as pl
from jax.experimental.pallas import tpu as pltpu
from jax.sharding import PartitionSpec as P

TILE = 128
COPIES = 14


def exchange_kernel(x_ref, g_ref, send_sems, recv_sems, local_sem):
    strip = x_ref.shape[2]
    half = strip // 2
    s = lax.axis_index("src")
    r = lax.axis_index("rcv")
    a = s + 1 - 2 * lax.rem(s, 2)
    b = lax.rem(s + 2, 4)
    d = 3 - s
    to_x, to_y, to_sibling = {"src": a}, {"src": b}, {"rcv": 1 - r}
    home = r == s // 2

    def place(u, t, rows=(0, strip), cols=(0, strip)):
        return g_ref.at[
            :,
            pl.ds(pl.multiple_of(u * strip + rows[0], half), rows[1]),
            pl.ds(pl.multiple_of(t * strip + cols[0], half), cols[1]),
        ]

    def own(t, rows=(0, strip), cols=(0, strip)):
        return x_ref.at[
            0,
            :,
            pl.ds(rows[0], rows[1]),
            pl.ds(pl.multiple_of(lax.rem(t, 2) * strip + cols[0], half), cols[1]),
        ]

    def copy(number, source, target, device):
        return pltpu.make_async_remote_copy(
            src_ref=source,
            dst_ref=target,
            send_sem=send_sems.at[number],
            recv_sem=recv_sems.at[number],
            device_id=device,
            device_id_type=pl.DeviceIdType.MESH,
        )

    def arrive(number, target, device):
        copy(number, target, target, device).wait_recv()

    lower, upper = (0, half), (half, half)
    barrier = pltpu.get_barrier_semaphore()
    for device in (to_x, to_y, to_sibling):
        pl.semaphore_signal(barrier, inc=1, device_id=device, device_id_type=pl.DeviceIdType.MESH)
    pl.semaphore_wait(barrier, 3)

    def own_place(core):
        return g_ref.at[
            :,
            pl.ds(pl.multiple_of(s * strip, strip), strip),
            pl.ds(pl.multiple_of(core * 2 * strip, strip), 2 * strip),
        ]

    @pl.when(home)
    def _():
        sends = [
            copy(1, own(s, upper), place(s, s, upper), to_x),
            copy(3, own(s, lower), place(s, s, lower), to_y),
            copy(2, own(s, lower), place(s, s, lower), to_x),
            copy(4, own(s, upper), place(s, s, upper), to_y),
            copy(5, own(a), place(s, a), to_y),
            copy(0, x_ref.at[0], own_place(r), to_sibling),
        ]
        for send in sends:
            send.start()
        local = pltpu.make_async_copy(x_ref.at[0], own_place(r), local_sem)
        local.start()
        arrive(1, place(a, a, upper), to_x)
        forward = copy(6, place(a, a, upper), place(a, a, upper), to_y)
        forward.start()
        arrive(9, place(b, a, cols=upper), to_y)
        share = copy(11, place(b, a, cols=upper), place(b, a, cols=upper), to_sibling)
        share.start()
        arrive(0, own_place(1 - r), to_sibling)
        arrive(2, place(a, a, lower), to_x)
        arrive(12, place(a, d), to_sibling)
        arrive(13, place(a, b, lower), to_sibling)
        local.wait()
        for send in sends + [forward, share]:
            send.wait_send()

    @pl.when(jnp.logical_not(home))
    def _():
        sends = [
            copy(9, own(d, cols=upper), place(s, d, cols=upper), to_y),
            copy(7, own(b), place(s, b), to_x),
            copy(8, own(d, lower), place(s, d, lower), to_x),
            copy(0, x_ref.at[0], own_place(r), to_sibling),
        ]
        for send in sends:
            send.start()
        local = pltpu.make_async_copy(x_ref.at[0], own_place(r), local_sem)
        local.start()
        arrive(3, place(b, b, lower), to_y)
        forward = copy(10, place(b, b, lower), place(b, b, lower), to_x)
        forward.start()
        arrive(7, place(a, d), to_x)
        share = copy(12, place(a, d), place(a, d), to_sibling)
        share.start()
        arrive(8, place(a, b, lower), to_x)
        share_half = copy(13, place(a, b, lower), place(a, b, lower), to_sibling)
        share_half.start()
        arrive(0, own_place(1 - r), to_sibling)
        arrive(11, place(b, a, cols=upper), to_sibling)
        arrive(4, place(b, b, upper), to_y)
        arrive(5, place(b, d), to_y)
        arrive(6, place(d, d, upper), to_y)
        arrive(10, place(d, d, lower), to_x)
        local.wait()
        for send in sends + [forward, share, share_half]:
            send.wait_send()


def exchange(recorded):
    strip = recorded.shape[2]
    whole = 4 * strip
    return pl.pallas_call(
        exchange_kernel,
        out_shape=jax.ShapeDtypeStruct((2, whole, whole), recorded.dtype),
        in_specs=[pl.BlockSpec(memory_space=pl.ANY)],
        out_specs=pl.BlockSpec(memory_space=pl.ANY),
        scratch_shapes=[
            pltpu.SemaphoreType.DMA((COPIES,)),
            pltpu.SemaphoreType.DMA((COPIES,)),
            pltpu.SemaphoreType.DMA,
        ],
        compiler_params=pltpu.CompilerParams(collective_id=0, has_side_effects=True),
        name="exchange",
    )(recorded)


def apply_kernel(
    row_tiles, col_tiles, blocks, mixed, aperture, straight, places, left_ref, *refs
):
    if mixed:
        column_ref, row_ref, out_ref, lhs, rhs, acc = refs
    else:
        column_ref, out_ref, lhs, rhs, acc = refs
    j = pl.program_id(0)

    def span(block, count):
        return pl.ds(pl.multiple_of(block * (2 * TILE), 2 * TILE), count * 2 * TILE)

    @pl.when(j == 0)
    def _():
        def interleave(k, carry):
            for c in range(2):
                lhs[:, pl.ds(pl.multiple_of((2 * k + c) * TILE, TILE), TILE)] = left_ref[
                    c, :, pl.ds(pl.multiple_of(k * TILE, TILE), TILE)
                ]
            return carry

        lax.fori_loop(0, blocks, interleave, 0)

    def build(k, carry):
        here = pl.ds(pl.multiple_of(k * TILE, TILE), TILE)
        first = pl.ds(pl.multiple_of(k * 2 * TILE, TILE), TILE)
        second = pl.ds(pl.multiple_of(k * 2 * TILE + TILE, TILE), TILE)

        def fill(real, imag):
            rhs[first, :TILE] = real
            rhs[first, TILE:] = imag
            rhs[second, :TILE] = -imag
            rhs[second, TILE:] = real

        if not mixed:
            fill(column_ref[0, here, :], column_ref[1, here, :])
            return carry
        as_is = straight[k * col_tiles + j] == 1

        @pl.when(as_is)
        def _():
            fill(column_ref[0, here, :], column_ref[1, here, :])

        @pl.when(jnp.logical_not(as_is))
        def _():
            fill(row_ref[0, :, here].T, row_ref[1, :, here].T)

        return carry

    lax.fori_loop(0, blocks, build, 0)

    def source_tile(i, carry):
        rows = pl.ds(pl.multiple_of(i * TILE, TILE), TILE)
        field = (i * col_tiles + j) * 3
        lo, extent, taper = aperture[field], aperture[field + 1], aperture[field + 2]
        acc[...] = jnp.zeros_like(acc)
        position = lo + taper
        inner = extent - 2 * taper
        size = 1
        while size * 2 <= blocks:
            size *= 2
        while size:
            present = lax.rem(inner // size, 2)

            @pl.when(present == 1)
            def _(size=size, position=position):
                part = span(position, size)
                acc[...] += jnp.dot(
                    lhs[rows, part], rhs[part, :], preferred_element_type=jnp.float32
                )

            position = position + present * size
            size //= 2
        for width in (1, 2):

            @pl.when(taper == width)
            def _(width=width):
                total = acc[...]
                for p in range(width):
                    weight = np.float32(p + 1) / np.float32(width + 1)
                    for block in (lo + p, lo + extent - 1 - p):
                        part = span(block, 1)
                        scaled = (lhs[rows, part].astype(jnp.float32) * weight).astype(jnp.bfloat16)
                        total += jnp.dot(scaled, rhs[part, :], preferred_element_type=jnp.float32)
                acc[...] = total

        out_ref[0, rows, :] = acc[:, :TILE]
        out_ref[1, rows, :] = acc[:, TILE:]
        return carry

    lax.fori_loop(0, row_tiles, source_tile, 0)


def apply(aperture, straight, places, left, column, row, own_rows, own_cols):
    whole = column.shape[1]
    blocks = whole // TILE
    row_tiles, col_tiles = own_rows // TILE, own_cols // TILE
    mixed = row is not None
    in_specs = [
        pl.BlockSpec(
            (2, own_rows, whole), lambda j, f, h, p: (0, p[0], 0), pipeline_mode=pl.Buffered(1)
        ),
        pl.BlockSpec((2, whole, TILE), lambda j, f, h, p: (0, 0, p[1] + j)),
    ]
    operands = [left, column]
    if mixed:
        in_specs.append(pl.BlockSpec((2, TILE, whole), lambda j, f, h, p: (0, p[1] + j, 0)))
        operands.append(row)
    flops = 8 * own_rows * own_cols * whole
    return pl.pallas_call(
        functools.partial(apply_kernel, row_tiles, col_tiles, blocks, mixed),
        out_shape=jax.ShapeDtypeStruct((2, own_rows, own_cols), jnp.float32),
        grid_spec=pltpu.PrefetchScalarGridSpec(
            num_scalar_prefetch=3,
            grid=(col_tiles,),
            in_specs=in_specs,
            out_specs=pl.BlockSpec((2, own_rows, TILE), lambda j, f, h, p: (0, 0, j)),
            scratch_shapes=[
                pltpu.VMEM((own_rows, 2 * whole), jnp.bfloat16),
                pltpu.VMEM((2 * whole, 2 * TILE), jnp.bfloat16),
                pltpu.VMEM((TILE, 2 * TILE), jnp.float32),
            ],
        ),
        compiler_params=pltpu.CompilerParams(vmem_limit_bytes=58 * 1024 * 1024),
        cost_estimate=pl.CostEstimate(
            flops=flops, bytes_accessed=40 * own_rows * whole, transcendentals=0
        ),
        name="apply_apertures",
    )(aperture.reshape(-1), straight.reshape(-1), places, *operands)


def held_straight(s, strip, first_tile, col_tiles):
    a, b, d = s + 1 - 2 * (s % 2), (s + 2) % 4, 3 - s
    per_half = strip // TILE // 2
    q = (jnp.arange(8 * per_half, dtype=jnp.int32) // per_half)[:, None]
    j = ((first_tile + jnp.arange(col_tiles, dtype=jnp.int32)) // per_half)[None, :]
    u, u_half, t, t_half = q // 2, q % 2, j // 2, j % 2
    held = (u == s) | ((u == t) & (t != s)) | ((u == a) & (t == d)) | ((u == b) & (t == d))
    held = held | ((u == a) & (t == b) & (u_half == 0)) | ((u == b) & (t == a) & (t_half == 1))
    return held.astype(jnp.int32)


def shards(square, recorded, aperture):
    own_rows, own_cols = recorded.shape[2], recorded.shape[3]
    row_tiles, col_tiles = own_rows // TILE, own_cols // TILE
    if square:
        s = lax.axis_index("src").astype(jnp.int32)
        first_tile = lax.axis_index("rcv").astype(jnp.int32) * col_tiles
        whole = exchange(recorded)
        straight = held_straight(s, own_rows, first_tile, col_tiles)
        places = jnp.stack([s, first_tile])
        out = apply(aperture, straight, places, whole, whole, whole, own_rows, own_cols)
        return out[None]
    places = jnp.zeros((2,), jnp.int32)
    straight = jnp.ones((1,), jnp.int32)
    left = lax.all_gather(recorded, "rcv", axis=3, tiled=True)
    column = lax.all_gather(recorded, "src", axis=2, tiled=True)
    outs = [
        apply(aperture, straight, places, left[f], column[f], None, own_rows, own_cols)
        for f in range(recorded.shape[0])
    ]
    return jnp.stack(outs)


def solution(mesh):
    square = mesh.shape["src"] == 4 and mesh.shape["rcv"] == 2
    in_specs = (P("grp", None, "src", "rcv"), P(("grp", "src"), "rcv", None))
    out_specs = P("grp", None, "src", "rcv")
    return jax.shard_map(
        functools.partial(shards, square),
        mesh=mesh,
        in_specs=in_specs,
        out_specs=out_specs,
        check_vma=False,
    )
```

time: 2210 us -> 434 us (0.20)
  the two profiles are of different devices: /device:TPU:1 before, /device:TPU:8 now
where the time goes in v1:
time: 434 us; the launch traced here: 430 us
  Pallas kernels  427 us (98%)
    pallas_call x1, Pallas kernels, exchange(): pl.pallas_call(exchange_kernel, out_shape=jax.ShapeDtypeStruct((2, whole,...  257 us
    pallas_call x1, Pallas kernels, apply(): pl.pallas_call(functools.partial(apply_kernel, row_tiles, col_tiles, bloc...  170 us

profile of v1, /device:TPU:8, one launch (start us, length us, event | category | flops | bytes accessed | tf_op | source)
XLA Modules:
  0.0 430.4 jit_solution(10844095355039059415)
XLA Ops:
  0.0 0.7 pad_add_fusion.places
  0.8 0.1 or_convert_fusion
  0.9 0.1 copy.5
  1.0 0.7 reshape.200.straight
  1.6 0.8 copy.4
  2.5 0.8 reshape.196.aperture
  3.2 257.0 %exchange.1.left_ref.refs_0_.refs_1_ = bf16[2,4096,4096]{2,1,0:T(8,128)(2,1)} custom-call(bf16[1,2,1024,2048]{3,2,1,0:T(8,128)(2,1)} %x_ref.1), custom_call_target="tpu_custom_call" | custom-call | tf_op jit(solution)/shard_map/exchange/pallas_call | solution.py:130
  260.3 170.1 %apply_apertures.1 = f32[2,1024,2048]{2,1,0:T(8,128)} custom-call(s32[384]{0:T(512)} %reshape.196.aperture, s32[512]{0:T(512)} %reshape.200.straight, s32[2]{0:T(128)} %pad_add_fusion.places, bf16[2,4096,4096]{2,1,0:T(8,128)(2,1)} %exchange.1.left_ref.refs_0_.refs_1_, bf16[2,4096,4096]{2,1,0:T(8,128)(2,1)} %exchange.1.left_ref.refs_0_.refs_1_, ...), custom_call_target="tpu_custom_call" | custom-call | flops 68719476736 | bytes 167772160 | tf_op jit(solution)/shard_map/apply_apertures/pallas_call | solution.py:254
  (7 shorter events, 0.1 us)

commit v2 on v1

--- a/solution.py
+++ b/solution.py
@@ -12,9 +12,11 @@
 COPIES = 14
 
 
-def exchange_kernel(x_ref, g_ref, send_sems, recv_sems, local_sem):
+def fused_kernel(x_ref, w_ref, out_ref, g_ref, lhs, raw, rhs, send_sems, recv_sems, local_sem):
     strip = x_ref.shape[2]
     half = strip // 2
+    tiles = strip // TILE
+    depth = 2 * strip
     s = lax.axis_index("src")
     r = lax.axis_index("rcv")
     a = s + 1 - 2 * lax.rem(s, 2)
@@ -51,11 +53,87 @@
     def arrive(number, target, device):
         copy(number, target, target, device).wait_recv()
 
-    lower, upper = (0, half), (half, half)
-    barrier = pltpu.get_barrier_semaphore()
-    for device in (to_x, to_y, to_sibling):
-        pl.semaphore_signal(barrier, inc=1, device_id=device, device_id_type=pl.DeviceIdType.MESH)
-    pl.semaphore_wait(barrier, 3)
+    def load(source, rows=(0, strip), cols=(0, strip)):
+        target = raw.at[:, pl.ds(rows[0], rows[1]), pl.ds(cols[0], cols[1])]
+        fetch = pltpu.make_async_copy(source, target, local_sem)
+        fetch.start()
+        fetch.wait()
+
+    def fill_left(u):
+        def one(k, carry):
+            for c in range(2):
+                lane = pl.multiple_of(u * depth + (2 * k + c) * TILE, TILE)
+                lhs[:, pl.ds(lane, TILE)] = raw[
+                    c, :strip, pl.ds(pl.multiple_of(k * TILE, TILE), TILE)
+                ]
+            return carry
+
+        lax.fori_loop(0, tiles, one, 0)
+
+    def at(tile, offset=0):
+        return pl.ds(pl.multiple_of(tile * TILE + offset, TILE), TILE)
+
+    def build(j, low, high, flip, offset):
+        def one(k, carry):
+            row, col = (j, k) if flip else (k, j)
+            real = raw[0, at(row, offset), at(col)]
+            imag = raw[1, at(row, offset), at(col)]
+            if flip:
+                real, imag = real.T, imag.T
+            first, second = at(2 * k), at(2 * k + 1)
+            rhs[first, :TILE] = real
+            rhs[first, TILE:] = imag
+            rhs[second, :TILE] = -imag
+            rhs[second, TILE:] = real
+            return carry
+
+        lax.fori_loop(low, high, one, 0)
+
+    def multiply(u, t, mode, first):
+        left = pl.ds(pl.multiple_of(u * depth, depth), depth)
+        group = 2 * TILE if tiles % 2 == 0 else TILE
+        side = lax.rem(t, 2)
+
+        def column(j, carry):
+            if mode == "mixed home":
+
+                @pl.when(j < tiles // 2)
+                def _():
+                    build(j, 0, tiles, True, 0)
+
+                @pl.when(j >= tiles // 2)
+                def _():
+                    build(j, 0, tiles, False, half)
+
+            elif mode == "mixed other":
+                build(j, 0, tiles // 2, False, 0)
+                build(j, tiles // 2, tiles, True, half)
+            else:
+                build(j, 0, tiles, mode == "flip", 0)
+            lanes = at(side * tiles + j)
+
+            def source(i, carry):
+                rows = pl.ds(pl.multiple_of(i * group, group), group)
+                parts = []
+                for n in range(group // TILE):
+                    tile = i * (group // TILE) + n
+                    weight = w_ref[pl.ds(tile * 2 * tiles + side * tiles + j, 1), left]
+                    piece = lhs[pl.ds(pl.multiple_of(tile * TILE, TILE), TILE), left]
+                    parts.append((piece.astype(jnp.float32) * weight).astype(jnp.bfloat16))
+                scaled = jnp.concatenate(parts, axis=0)
+                product = jnp.dot(scaled, rhs[...], preferred_element_type=jnp.float32)
+                if first:
+                    out_ref[0, rows, lanes] = product[:, :TILE]
+                    out_ref[1, rows, lanes] = product[:, TILE:]
+                else:
+                    out_ref[0, rows, lanes] += product[:, :TILE]
+                    out_ref[1, rows, lanes] += product[:, TILE:]
+                return carry
+
+            lax.fori_loop(0, strip // group, source, 0)
+            return carry
+
+        lax.fori_loop(0, tiles, column, 0)
 
     def own_place(core):
         return g_ref.at[
@@ -64,82 +142,146 @@
             pl.ds(pl.multiple_of(core * 2 * strip, strip), 2 * strip),
         ]
 
+    def load_mixed():
+        load(place(a, b, lower), rows=(0, half))
+        load(place(b, a, cols=upper), rows=(half, strip), cols=upper)
+
+    lower, upper = (0, half), (half, half)
+    barrier = pltpu.get_barrier_semaphore()
+    for device in (to_x, to_y, to_sibling):
+        pl.semaphore_signal(barrier, inc=1, device_id=device, device_id_type=pl.DeviceIdType.MESH)
+    pl.semaphore_wait(barrier, 3)
+
     @pl.when(home)
     def _():
         sends = [
+            copy(0, x_ref.at[0], own_place(r), to_sibling),
             copy(1, own(s, upper), place(s, s, upper), to_x),
             copy(3, own(s, lower), place(s, s, lower), to_y),
             copy(2, own(s, lower), place(s, s, lower), to_x),
             copy(4, own(s, upper), place(s, s, upper), to_y),
             copy(5, own(a), place(s, a), to_y),
-            copy(0, x_ref.at[0], own_place(r), to_sibling),
         ]
         for send in sends:
             send.start()
-        local = pltpu.make_async_copy(x_ref.at[0], own_place(r), local_sem)
-        local.start()
+        load(own(s))
+        fill_left(s)
+        multiply(s, s, "as is", True)
+        load(own(a))
+        fill_left(a)
+        multiply(s, a, "as is", True)
         arrive(1, place(a, a, upper), to_x)
         forward = copy(6, place(a, a, upper), place(a, a, upper), to_y)
         forward.start()
+        multiply(a, s, "flip", False)
+        arrive(0, own_place(1 - r), to_sibling)
+        load(place(s, b))
+        fill_left(b)
+        multiply(b, s, "flip", False)
         arrive(9, place(b, a, cols=upper), to_y)
         share = copy(11, place(b, a, cols=upper), place(b, a, cols=upper), to_sibling)
         share.start()
-        arrive(0, own_place(1 - r), to_sibling)
+        load(place(s, d))
+        fill_left(d)
+        multiply(d, s, "flip", False)
         arrive(2, place(a, a, lower), to_x)
+        load(place(a, a))
+        multiply(a, a, "as is", False)
         arrive(12, place(a, d), to_sibling)
+        load(place(a, d))
+        multiply(d, a, "flip", False)
         arrive(13, place(a, b, lower), to_sibling)
-        local.wait()
+        load_mixed()
+        multiply(b, a, "mixed home", False)
         for send in sends + [forward, share]:
             send.wait_send()
 
     @pl.when(jnp.logical_not(home))
     def _():
         sends = [
+            copy(0, x_ref.at[0], own_place(r), to_sibling),
             copy(9, own(d, cols=upper), place(s, d, cols=upper), to_y),
             copy(7, own(b), place(s, b), to_x),
             copy(8, own(d, lower), place(s, d, lower), to_x),
-            copy(0, x_ref.at[0], own_place(r), to_sibling),
         ]
         for send in sends:
             send.start()
-        local = pltpu.make_async_copy(x_ref.at[0], own_place(r), local_sem)
-        local.start()
+        arrive(0, own_place(1 - r), to_sibling)
+        load(place(s, a))
+        fill_left(a)
+        load(place(s, s))
+        fill_left(s)
         arrive(3, place(b, b, lower), to_y)
         forward = copy(10, place(b, b, lower), place(b, b, lower), to_x)
         forward.start()
+        load(own(b))
+        fill_left(b)
+        multiply(s, b, "as is", True)
+        load(own(d))
+        fill_left(d)
+        multiply(s, d, "as is", True)
+        arrive(4, place(b, b, upper), to_y)
+        load(place(b, b))
+        multiply(b, b, "as is", False)
         arrive(7, place(a, d), to_x)
         share = copy(12, place(a, d), place(a, d), to_sibling)
         share.start()
+        load(place(a, d))
+        multiply(a, d, "as is", False)
         arrive(8, place(a, b, lower), to_x)
         share_half = copy(13, place(a, b, lower), place(a, b, lower), to_sibling)
         share_half.start()
-        arrive(0, own_place(1 - r), to_sibling)
         arrive(11, place(b, a, cols=upper), to_sibling)
-        arrive(4, place(b, b, upper), to_y)
+        load_mixed()
+        multiply(a, b, "mixed other", False)
         arrive(5, place(b, d), to_y)
+        load(place(b, d))
+        multiply(b, d, "as is", False)
+        multiply(d, b, "flip", False)
         arrive(6, place(d, d, upper), to_y)
         arrive(10, place(d, d, lower), to_x)
-        local.wait()
+        load(place(d, d))
+        multiply(d, d, "as is", False)
         for send in sends + [forward, share, share_half]:
             send.wait_send()
 
 
-def exchange(recorded):
-    strip = recorded.shape[2]
-    whole = 4 * strip
-    return pl.pallas_call(
-        exchange_kernel,
-        out_shape=jax.ShapeDtypeStruct((2, whole, whole), recorded.dtype),
-        in_specs=[pl.BlockSpec(memory_space=pl.ANY)],
-        out_specs=pl.BlockSpec(memory_space=pl.ANY),
+def fused(recorded, weights):
+    rows, cols = recorded.shape[2], recorded.shape[3]
+    whole = 4 * rows
+    out, _ = pl.pallas_call(
+        fused_kernel,
+        out_shape=(
+            jax.ShapeDtypeStruct((2, rows, cols), jnp.float32),
+            jax.ShapeDtypeStruct((2, whole, whole), recorded.dtype),
+        ),
+        in_specs=[pl.BlockSpec(memory_space=pl.ANY), pl.BlockSpec(memory_space=pltpu.VMEM)],
+        out_specs=(pl.BlockSpec(memory_space=pltpu.VMEM), pl.BlockSpec(memory_space=pl.ANY)),
         scratch_shapes=[
+            pltpu.VMEM((rows, 2 * whole), jnp.bfloat16),
+            pltpu.VMEM((2, rows + rows // 2, rows), jnp.bfloat16),
+            pltpu.VMEM((2 * rows, 2 * TILE), jnp.bfloat16),
             pltpu.SemaphoreType.DMA((COPIES,)),
             pltpu.SemaphoreType.DMA((COPIES,)),
             pltpu.SemaphoreType.DMA,
         ],
-        compiler_params=pltpu.CompilerParams(collective_id=0, has_side_effects=True),
-        name="exchange",
-    )(recorded)
+        compiler_params=pltpu.CompilerParams(
+            collective_id=0, has_side_effects=True, vmem_limit_bytes=60 * 1024 * 1024
+        ),
+        cost_estimate=pl.CostEstimate(
+            flops=8 * rows * cols * whole, bytes_accessed=40 * rows * whole, transcendentals=0
+        ),
+        name="exchange_and_multiply",
+    )(recorded, weights)
+    return out
+
+
+def tile_weights(aperture, blocks):
+    offset = jnp.arange(blocks, dtype=jnp.int32)[None, None, :] - aperture[..., 0:1]
+    extent = aperture[..., 1:2]
+    margin = jnp.minimum(offset, extent - 1 - offset)
+    ramp = (margin + 1).astype(jnp.float32) / (aperture[..., 2:3] + 1).astype(jnp.float32)
+    return jnp.where((offset >= 0) & (offset < extent), jnp.minimum(1.0, ramp), 0.0)
 
 
 def apply_kernel(
@@ -273,27 +415,13 @@
     )(aperture.reshape(-1), straight.reshape(-1), places, *operands)
 
 
-def held_straight(s, strip, first_tile, col_tiles):
-    a, b, d = s + 1 - 2 * (s % 2), (s + 2) % 4, 3 - s
-    per_half = strip // TILE // 2
-    q = (jnp.arange(8 * per_half, dtype=jnp.int32) // per_half)[:, None]
-    j = ((first_tile + jnp.arange(col_tiles, dtype=jnp.int32)) // per_half)[None, :]
-    u, u_half, t, t_half = q // 2, q % 2, j // 2, j % 2
-    held = (u == s) | ((u == t) & (t != s)) | ((u == a) & (t == d)) | ((u == b) & (t == d))
-    held = held | ((u == a) & (t == b) & (u_half == 0)) | ((u == b) & (t == a) & (t_half == 1))
-    return held.astype(jnp.int32)
-
-
 def shards(square, recorded, aperture):
     own_rows, own_cols = recorded.shape[2], recorded.shape[3]
     row_tiles, col_tiles = own_rows // TILE, own_cols // TILE
     if square:
-        s = lax.axis_index("src").astype(jnp.int32)
-        first_tile = lax.axis_index("rcv").astype(jnp.int32) * col_tiles
-        whole = exchange(recorded)
-        straight = held_straight(s, own_rows, first_tile, col_tiles)
-        places = jnp.stack([s, first_tile])
-        out = apply(aperture, straight, places, whole, whole, whole, own_rows, own_cols)
+        weights = tile_weights(aperture, 4 * row_tiles)
+        weights = jnp.repeat(weights.reshape(row_tiles * col_tiles, -1), 2 * TILE, axis=1)
+        out = fused(recorded, weights)
         return out[None]
     places = jnp.zeros((2,), jnp.int32)
     straight = jnp.ones((1,), jnp.int32)

time: 434 us -> 229 us (0.53)
  the two profiles are of different devices: /device:TPU:8 before, /device:TPU:1 now
where the time goes in v2:
time: 229 us
  Pallas kernels  210 us (92%)
  local copies, waits for them, and re-layouts  18 us (8%)
    pallas_call x1, Pallas kernels, fused(): pl.pallas_call(fused_kernel, out_shape=(jax.ShapeDtypeStruct((2, rows, co...  210 us
    unnamed x2, local copies, waits for them, and re-layouts  17.1 us

profile of v2, /device:TPU:1, one launch (start us, length us, event | category | flops | bytes accessed | tf_op | source)
XLA Modules:
  0.0 228.8 jit_solution(2657218772364499786)
XLA Ops:
  0.0 0.7 fusion.8
  0.7 0.1 sub.31
  0.8 0.1 sub.35
  0.9 0.1 div.11
  1.0 0.1 lt.11
  1.0 0.1 fusion.4
  1.2 0.6 broadcast_in_dim.12
  1.8 5.3 %copy.3 = f32[16,8,32,256]{3,1,2,0:T(8,128)} copy(f32[16,8,32,256]{3,2,1,0:T(8,128)S(1)} %bitcast.12) | data formatting | bytes 8388608
  7.1 209.8 %exchange_and_multiply.1 = (f32[2,1024,2048]{2,1,0:T(8,128)}, bf16[2,4096,4096]{2,1,0:T(8,128)(2,1)}) custom-call(bf16[1,2,1024,2048]{3,2,1,0:T(8,128)(2,1)} %x_ref.1, f32[128,8192]{1,0:T(8,128)} %bitcast.13), custom_call_target="tpu_custom_call" | custom-call | flops 68719476736 | bytes 167772160 | tf_op jit(solution)/shard_map/exchange_and_multiply/pallas_call | solution.py:252
  217.0 11.8 %copy.5 = f32[1,2,1024,2048]{3,2,1,0:T(8,128)} copy(f32[1,2,1024,2048]{3,2,1,0:T(8,128)} %bitcast.11) | data formatting | bytes 33554432

commit v3 on v2

--- a/solution.py
+++ b/solution.py
@@ -9,12 +9,12 @@
 from jax.sharding import PartitionSpec as P
 
 TILE = 128
-COPIES = 14
+COPIES = 26
 
 
 def fused_kernel(x_ref, w_ref, out_ref, g_ref, lhs, raw, rhs, send_sems, recv_sems, local_sem):
     strip = x_ref.shape[2]
-    half = strip // 2
+    half, band = strip // 2, strip // 4
     tiles = strip // TILE
     depth = 2 * strip
     s = lax.axis_index("src")
@@ -28,8 +28,8 @@
     def place(u, t, rows=(0, strip), cols=(0, strip)):
         return g_ref.at[
             :,
-            pl.ds(pl.multiple_of(u * strip + rows[0], half), rows[1]),
-            pl.ds(pl.multiple_of(t * strip + cols[0], half), cols[1]),
+            pl.ds(pl.multiple_of(u * strip + rows[0], TILE), rows[1]),
+            pl.ds(pl.multiple_of(t * strip + cols[0], TILE), cols[1]),
         ]
 
     def own(t, rows=(0, strip), cols=(0, strip)):
@@ -37,7 +37,7 @@
             0,
             :,
             pl.ds(rows[0], rows[1]),
-            pl.ds(pl.multiple_of(lax.rem(t, 2) * strip + cols[0], half), cols[1]),
+            pl.ds(pl.multiple_of(lax.rem(t, 2) * strip + cols[0], TILE), cols[1]),
         ]
 
     def copy(number, source, target, device):
@@ -90,7 +90,6 @@
         lax.fori_loop(low, high, one, 0)
 
     def multiply(u, t, mode, first):
-        left = pl.ds(pl.multiple_of(u * depth, depth), depth)
         group = 2 * TILE if tiles % 2 == 0 else TILE
         side = lax.rem(t, 2)
 
@@ -108,6 +107,10 @@
             elif mode == "mixed other":
                 build(j, 0, tiles // 2, False, 0)
                 build(j, tiles // 2, tiles, True, half)
+            elif mode == "diagonal":
+                stair = (j // (tiles // 4) + 1) * (tiles // 4)
+                build(j, 0, stair, False, 0)
+                build(j, stair, tiles, True, 0)
             else:
                 build(j, 0, tiles, mode == "flip", 0)
             lanes = at(side * tiles + j)
@@ -117,9 +120,14 @@
                 parts = []
                 for n in range(group // TILE):
                     tile = i * (group // TILE) + n
-                    weight = w_ref[pl.ds(tile * 2 * tiles + side * tiles + j, 1), left]
-                    piece = lhs[pl.ds(pl.multiple_of(tile * TILE, TILE), TILE), left]
-                    parts.append((piece.astype(jnp.float32) * weight).astype(jnp.bfloat16))
+                    first_weight = ((tile * 2 + side) * tiles + j) * 4 * tiles + u * tiles
+                    blocks = []
+                    for k in range(tiles):
+                        lane = pl.multiple_of(u * depth + k * 2 * TILE, 2 * TILE)
+                        piece = lhs[pl.ds(pl.multiple_of(tile * TILE, TILE), TILE), pl.ds(lane, 2 * TILE)]
+                        weight = w_ref[first_weight + k]
+                        blocks.append((piece.astype(jnp.float32) * weight).astype(jnp.bfloat16))
+                    parts.append(jnp.concatenate(blocks, axis=1))
                 scaled = jnp.concatenate(parts, axis=0)
                 product = jnp.dot(scaled, rhs[...], preferred_element_type=jnp.float32)
                 if first:
@@ -135,6 +143,16 @@
 
         lax.fori_loop(0, tiles, column, 0)
 
+    def stair(u, i):
+        return place(u, u, (i * band, band), (i * band, strip - i * band))
+
+    def own_stair(i):
+        return own(s, (i * band, band), (i * band, strip - i * band))
+
+    def load_diagonal(u):
+        for i in range(4):
+            load(stair(u, i), (i * band, band), (i * band, strip - i * band))
+
     def own_place(core):
         return g_ref.at[
             :,
@@ -156,10 +174,14 @@
     def _():
         sends = [
             copy(0, x_ref.at[0], own_place(r), to_sibling),
-            copy(1, own(s, upper), place(s, s, upper), to_x),
-            copy(3, own(s, lower), place(s, s, lower), to_y),
-            copy(2, own(s, lower), place(s, s, lower), to_x),
-            copy(4, own(s, upper), place(s, s, upper), to_y),
+            copy(15, own_stair(1), stair(s, 1), to_x),
+            copy(18, own_stair(0), stair(s, 0), to_y),
+            copy(16, own_stair(2), stair(s, 2), to_x),
+            copy(21, own_stair(3), stair(s, 3), to_y),
+            copy(14, own_stair(0), stair(s, 0), to_x),
+            copy(19, own_stair(1), stair(s, 1), to_y),
+            copy(17, own_stair(3), stair(s, 3), to_x),
+            copy(20, own_stair(2), stair(s, 2), to_y),
             copy(5, own(a), place(s, a), to_y),
         ]
         for send in sends:
@@ -170,9 +192,11 @@
         load(own(a))
         fill_left(a)
         multiply(s, a, "as is", True)
-        arrive(1, place(a, a, upper), to_x)
-        forward = copy(6, place(a, a, upper), place(a, a, upper), to_y)
-        forward.start()
+        forwards = []
+        for i in (1, 2):
+            arrive(14 + i, stair(a, i), to_x)
+            forwards.append(copy(21 + i, stair(a, i), stair(a, i), to_y))
+            forwards[-1].start()
         multiply(a, s, "flip", False)
         arrive(0, own_place(1 - r), to_sibling)
         load(place(s, b))
@@ -184,16 +208,17 @@
         load(place(s, d))
         fill_left(d)
         multiply(d, s, "flip", False)
-        arrive(2, place(a, a, lower), to_x)
-        load(place(a, a))
-        multiply(a, a, "as is", False)
+        arrive(14, stair(a, 0), to_x)
+        arrive(17, stair(a, 3), to_x)
+        load_diagonal(a)
+        multiply(a, a, "diagonal", False)
         arrive(12, place(a, d), to_sibling)
         load(place(a, d))
         multiply(d, a, "flip", False)
         arrive(13, place(a, b, lower), to_sibling)
         load_mixed()
         multiply(b, a, "mixed home", False)
-        for send in sends + [forward, share]:
+        for send in sends + forwards + [share]:
             send.wait_send()
 
     @pl.when(jnp.logical_not(home))
@@ -211,18 +236,21 @@
         fill_left(a)
         load(place(s, s))
         fill_left(s)
-        arrive(3, place(b, b, lower), to_y)
-        forward = copy(10, place(b, b, lower), place(b, b, lower), to_x)
-        forward.start()
+        forwards = []
+        for n, i in enumerate((0, 3)):
+            arrive(18 + i, stair(b, i), to_y)
+            forwards.append(copy(24 + n, stair(b, i), stair(b, i), to_x))
+            forwards[-1].start()
         load(own(b))
         fill_left(b)
         multiply(s, b, "as is", True)
         load(own(d))
         fill_left(d)
         multiply(s, d, "as is", True)
-        arrive(4, place(b, b, upper), to_y)
-        load(place(b, b))
-        multiply(b, b, "as is", False)
+        arrive(19, stair(b, 1), to_y)
+        arrive(20, stair(b, 2), to_y)
+        load_diagonal(b)
+        multiply(b, b, "diagonal", False)
         arrive(7, place(a, d), to_x)
         share = copy(12, place(a, d), place(a, d), to_sibling)
         share.start()
@@ -238,11 +266,13 @@
         load(place(b, d))
         multiply(b, d, "as is", False)
         multiply(d, b, "flip", False)
-        arrive(6, place(d, d, upper), to_y)
-        arrive(10, place(d, d, lower), to_x)
-        load(place(d, d))
-        multiply(d, d, "as is", False)
-        for send in sends + [forward, share, share_half]:
+        arrive(22, stair(d, 1), to_y)
+        arrive(23, stair(d, 2), to_y)
+        arrive(24, stair(d, 0), to_x)
+        arrive(25, stair(d, 3), to_x)
+        load_diagonal(d)
+        multiply(d, d, "diagonal", False)
+        for send in sends + forwards + [share, share_half]:
             send.wait_send()
 
 
@@ -255,7 +285,7 @@
             jax.ShapeDtypeStruct((2, rows, cols), jnp.float32),
             jax.ShapeDtypeStruct((2, whole, whole), recorded.dtype),
         ),
-        in_specs=[pl.BlockSpec(memory_space=pl.ANY), pl.BlockSpec(memory_space=pltpu.VMEM)],
+        in_specs=[pl.BlockSpec(memory_space=pl.ANY), pl.BlockSpec(memory_space=pltpu.SMEM)],
         out_specs=(pl.BlockSpec(memory_space=pltpu.VMEM), pl.BlockSpec(memory_space=pl.ANY)),
         scratch_shapes=[
             pltpu.VMEM((rows, 2 * whole), jnp.bfloat16),
@@ -420,8 +450,7 @@
     row_tiles, col_tiles = own_rows // TILE, own_cols // TILE
     if square:
         weights = tile_weights(aperture, 4 * row_tiles)
-        weights = jnp.repeat(weights.reshape(row_tiles * col_tiles, -1), 2 * TILE, axis=1)
-        out = fused(recorded, weights)
+        out = fused(recorded, weights.reshape(-1))
         return out[None]
     places = jnp.zeros((2,), jnp.int32)
     straight = jnp.ones((1,), jnp.int32)

time: 229 us -> 218 us (0.952)
  Pallas kernels: 210 us -> 203 us
  local copies, waits for them, and re-layouts: 18 us -> 12.4 us
    pallas_call x1, Pallas kernels: 210 us -> 203 us  [fused(): pl.pallas_call(fused_kernel, out_shape=(jax.ShapeDtypeStruct((2, rows, co...]
    unnamed x2 -> x1, local copies, waits for them, and re-layouts: 17.1 us -> 11.8 us
where the time goes in v3:
time: 218 us; the launch traced here: 217 us
  Pallas kernels  203 us (93%)
  local copies, waits for them, and re-layouts  12.4 us (6%)
    pallas_call x1, Pallas kernels, fused(): pl.pallas_call(fused_kernel, out_shape=(jax.ShapeDtypeStruct((2, rows, co...  203 us
    unnamed x1, local copies, waits for them, and re-layouts  11.8 us

profile of v3, /device:TPU:1, one launch (start us, length us, event | category | flops | bytes accessed | tf_op | source)
XLA Modules:
  0.0 216.9 jit_solution(8347444508939140522)
XLA Ops:
  0.0 0.7 slice_bitcast_fusion.1
  0.7 0.1 lt.14
  0.8 0.1 lt.15
  0.9 0.1 sub.42
  1.0 0.1 sub.43
  1.1 0.1 iota_subtract_fusion
  1.1 0.1 sub.39
  1.2 0.1 div.14
  1.3 0.1 div.15
  1.4 0.6 fusion.4.w_ref
  2.0 203.1 %exchange_and_multiply.1 = (f32[2,1024,2048]{2,1,0:T(8,128)}, bf16[2,4096,4096]{2,1,0:T(8,128)(2,1)}) custom-call(bf16[1,2,1024,2048]{3,2,1,0:T(8,128)(2,1)} %x_ref.1, f32[4096]{0:T(1024)} %fusion.4.w_ref), custom_call_target="tpu_custom_call" | custom-call | flops 68719476736 | bytes 167772160 | tf_op jit(solution)/shard_map/exchange_and_multiply/pallas_call | solution.py:282
  205.1 11.8 %copy.4 = f32[1,2,1024,2048]{3,2,1,0:T(8,128)} copy(f32[1,2,1024,2048]{3,2,1,0:T(8,128)} %bitcast.9) | data formatting | bytes 33554432

commit v4 on v3

--- a/solution.py
+++ b/solution.py
@@ -87,10 +87,11 @@
             rhs[second, TILE:] = real
             return carry
 
-        lax.fori_loop(low, high, one, 0)
+        static = isinstance(low, int) and isinstance(high, int)
+        lax.fori_loop(low, high, one, 0, unroll=4 if static and (high - low) % 4 == 0 else 1)
 
     def multiply(u, t, mode, first):
-        group = 2 * TILE if tiles % 2 == 0 else TILE
+        group = 4 * TILE if tiles % 4 == 0 else TILE
         side = lax.rem(t, 2)
 
         def column(j, carry):

time: 218 us -> 186 us (0.85)
  Pallas kernels: 203 us -> 172 us
    pallas_call x1, Pallas kernels: 203 us -> 172 us  [fused(): pl.pallas_call(fused_kernel, out_shape=(jax.ShapeDtypeStruct((2, rows, co...]
where the time goes in v4:
time: 186 us
  Pallas kernels  172 us (92%)
  local copies, waits for them, and re-layouts  12.4 us (7%)
    pallas_call x1, Pallas kernels, fused(): pl.pallas_call(fused_kernel, out_shape=(jax.ShapeDtypeStruct((2, rows, co...  172 us
    unnamed x1, local copies, waits for them, and re-layouts  11.8 us

profile of v4, /device:TPU:1, one launch (start us, length us, event | category | flops | bytes accessed | tf_op | source)
XLA Modules:
  0.0 185.6 jit_solution(16125711706643732358)
XLA Ops:
  0.0 0.7 slice_bitcast_fusion.1
  0.7 0.1 lt.14
  0.8 0.1 lt.15
  0.9 0.1 sub.42
  1.0 0.1 sub.43
  1.1 0.1 iota_subtract_fusion
  1.1 0.1 sub.39
  1.2 0.1 div.14
  1.3 0.1 div.15
  1.4 0.6 fusion.4.w_ref
  2.0 171.8 %exchange_and_multiply.1 = (f32[2,1024,2048]{2,1,0:T(8,128)}, bf16[2,4096,4096]{2,1,0:T(8,128)(2,1)}) custom-call(bf16[1,2,1024,2048]{3,2,1,0:T(8,128)(2,1)} %x_ref.1, f32[4096]{0:T(1024)} %fusion.4.w_ref), custom_call_target="tpu_custom_call" | custom-call | flops 68719476736 | bytes 167772160 | tf_op jit(solution)/shard_map/exchange_and_multiply/pallas_call | solution.py:283
  173.8 11.8 %copy.4 = f32[1,2,1024,2048]{3,2,1,0:T(8,128)} copy(f32[1,2,1024,2048]{3,2,1,0:T(8,128)} %bitcast.9) | data formatting | bytes 33554432
